TPU v7x, 256 devices: a whole 4x4x8 slice. The times are simulated.
256 devices in a mesh: seq: 64 (over y, z, core), fsdp: 4 (over x).
Axes of the slice: x: 4, y: 4, z: 8, core: 2. Of those that a mesh axis runs over, the one named last changes fastest.
Arguments:
- tokens: bfloat16 [65536, 4096], P('seq', 'fsdp'), may hold values from -6 to 6
- projection: bfloat16 [3, 4096, 2048], P(None, 'seq', 'fsdp'), may hold values from -0.09375 to 0.09375
- log_decay: float32 [65536, 16], P('seq', 'fsdp'), may hold values from -2 to 0, as said below
Outputs:
- attended: bfloat16 [65536, 2048], P('seq', 'fsdp')
Inputs may be any that keep to these rules, and one draw needn't show every extreme that they name: `log_decay`: negative logarithms of decay factors, one for each position and head.
All inputs are finite; a program needn't handle non-finite values.
Results may differ from a plain program's by a relative error of at most 0.006.
Values may be sent and summed in bfloat16 or wider, within the bound.
No kernel may reach another device: no remote copies, remote signals or barrier semaphores. Data moves between devices by JAX's collectives and lax.ppermute only.
A program may use at most 64 MiB of HBM per device.

v0:
```python
import jax
import jax.numpy as jnp
from jax import lax
from jax.sharding import PartitionSpec as P

BLK = 512


def entering(part, axis, combine, identity):
    place = lax.axis_index(axis)
    gathered = jax.tree.map(lambda a: lax.all_gather(a, axis), part)
    state = jax.tree.map(lambda a, e: jnp.zeros_like(a) + jnp.asarray(e, a.dtype), part, identity)

    def one(hop, state):
        return combine(
            state, jax.tree.map(lambda a: lax.dynamic_index_in_dim(a, hop, 0, False), gathered)
        )

    return lax.fori_loop(0, place, one, state)


def local_states(key_vecs, value_vecs, decay):
    running = jnp.cumsum(decay, axis=1)
    last = running[:, -1]
    carried = key_vecs.astype(jnp.float32) * jnp.exp(last[:, None, :] - running)[..., None]
    fresh = jnp.einsum(
        "nshd,nshe->nhde", carried, value_vecs.astype(jnp.float32), precision=lax.Precision.HIGHEST
    )

    def advance(state, inputs):
        block_last, block_fresh = inputs
        return (jnp.exp(block_last)[:, None, None] * state + block_fresh, state)

    start = jnp.zeros(fresh.shape[1:], jnp.float32)
    final, before = lax.scan(advance, start, (last, fresh))
    leading = jnp.cumsum(last, axis=0) - last
    whole_decay = jnp.exp(jnp.sum(last, axis=0))
    return (final, before, leading, whole_decay)


def combine(earlier, later):
    return (earlier[0] * later[0], later[0][:, None, None] * earlier[1] + later[1])


def chain(key_raw, value_raw, decay, shaped):
    key_vecs = shaped(jax.nn.silu(key_raw).astype(jnp.bfloat16))
    value_vecs = shaped(value_raw.astype(jnp.bfloat16))
    final, before, leading, whole_decay = local_states(key_vecs, value_vecs, decay)
    identity = (jnp.ones_like(whole_decay), jnp.zeros_like(final))
    carry = entering((whole_decay, final), "seq", combine, identity)
    incoming = before + jnp.exp(leading)[:, :, None, None] * carry[1][None]
    return (key_vecs, value_vecs, incoming)


def attend_block(inputs):
    queries, key_vecs, value_vecs, decay, state = inputs
    running = jnp.cumsum(decay, axis=0)
    across = running.T
    gap = across[:, :, None] - across[:, None, :]
    lower = jnp.arange(gap.shape[1])[:, None] >= jnp.arange(gap.shape[2])[None, :]
    fading = jnp.exp(jnp.where(lower[None], gap, -1e30))
    scores = jnp.einsum("thd,shd->hts", queries, key_vecs, preferred_element_type=jnp.float32)
    weights = (fading * scores).astype(jnp.bfloat16)
    intra = jnp.einsum("hts,she->the", weights, value_vecs, preferred_element_type=jnp.float32)
    inter = jnp.exp(running)[:, :, None] * jnp.einsum(
        "thd,hde->the", queries.astype(jnp.float32), state, precision=lax.Precision.HIGHEST
    )
    mixed = intra + inter
    normed = mixed * lax.rsqrt(jnp.mean(mixed * mixed, axis=-1, keepdims=True) + 1e-06)
    return normed.astype(jnp.bfloat16)


def on_device(tokens, projection, log_decay):
    features = lax.all_gather(tokens, "fsdp", axis=1, tiled=True)
    rows = features.shape[0]
    heads = log_decay.shape[1]
    width = projection.shape[2]
    head = width // heads
    blocks = rows // BLK

    def shaped(matrix):
        return matrix.reshape(blocks, BLK, heads, head)

    decay = log_decay.reshape(blocks, BLK, heads)
    raw = jnp.einsum(
        "td,cdn->ctn",
        features,
        lax.all_gather(projection, "seq", axis=1, tiled=True),
        preferred_element_type=jnp.float32,
    )
    key_vecs, value_vecs, incoming = chain(raw[1], raw[2], decay, shaped)
    query_raw = raw[0]
    queries = shaped(jax.nn.silu(query_raw).astype(jnp.bfloat16))
    outputs = lax.map(attend_block, (queries, key_vecs, value_vecs, decay, incoming))
    return outputs.reshape(rows, width)


def solution(mesh):
    in_specs = (P("seq", "fsdp"), P(None, "seq", "fsdp"), P("seq", "fsdp"))
    out_specs = P("seq", "fsdp")
    return jax.shard_map(
        on_device, mesh=mesh, in_specs=in_specs, out_specs=out_specs, check_vma=False
    )
```

profile of v0, /device:TPU:249, one launch (start us, length us, event | category | flops | bytes accessed | tf_op | source)
XLA Modules:
  0.0 447.1 jit_solution(9601108571453135276)
XLA Ops:
  8.1 2.4 reduce-window.14
  11.5 83.5 %all-gather.8.cloned.1.call-done = bf16[1024,4096]{1,0:T(8,128)(2,1)} async-done(((bf16[1024,1024]{1,0:T(8,128)(2,1)}), bf16[1024,4096]{1,0:T(8,128)(2,1)}) %all-gather.8.cloned.1.call-update) | async-done | bytes 8388624 | tf_op jit(solution)/shard_map/all_gather | solution.py:74
  95.0 90.9 %all-gather.6.cloned.1.call-done = bf16[3,4096,512]{2,1,0:T(8,128)(2,1)} async-done(((bf16[3,64,512]{2,1,0:T(8,128)(2,1)}), bf16[3,4096,512]{2,1,0:T(8,128)(2,1)}) %all-gather.6.cloned.1.call-update) | async-done | bytes 12582928 | tf_op jit(solution)/shard_map/all_gather | solution.py:88
  185.9 17.3 %fusion.27 = f32[3,1024,512]{1,2,0:T(8,128)S(1)} fusion(bf16[3,4096,512]{2,1,0:T(8,128)(2,1)} %all-gather.6.cloned.1.call-done, bf16[1024,4096]{1,0:T(8,128)(2,1)} %all-gather.8.cloned.1.call-done), kind=kOutput, calls=%fused_computation.39 | convolution fusion | flops 12884901888 | bytes 27262976 | tf_op jit(solution)/shard_map/td,cdn->ctn/dot_general | solution.py:85
  203.3 1.8 fusion.35
  205.1 1.6 convert_element_type.24
  206.7 2.8 squeeze.42
  209.4 2.8 copy.51
  212.2 4.0 squeeze.41
  216.2 4.1 copy.49
  220.3 2.8 multiply_convert_fusion.2
  223.1 2.7 fusion.30
  228.3 124.5 %all-reduce = f32[256]{0:T(256)S(1)} all-reduce(f32[256]{0:T(256)S(1)} %exponential_dynamic-update-slice_fusion), channel_id=2, replica_groups=mesh['seq'=64,'fsdp'=4] {'seq'}, use_global_device_ids=true, to_apply=%add | all-reduce | flops 256 | bytes 2048
  353.0 1.2 copy.54
  354.2 69.7 %while.35 = (s32[]{:T(128)}, f32[4,128,128]{2,1,0:T(8,128)S(1)}, s32[]{:T(128)}, f32[64,4]{1,0:T(8,128)S(1)}, f32[64,4,128,128]{3,2,1,0:T(8,128)}, /*index=5*/s32[]{:T(128)}, s32[]{:T(128)}, s32[]{:T(128)}) while((s32[]{:T(128)}, f32[4,128,128]{2,1,0:T(8,128)S(1)}, s32[]{:T(128)}, f32[64,4]{1,0:T(8,128)S(1)}, f32[64,4,128,128]{3,2,1,0:T(8,128)}, ...), condition=%wide.region_7.8_spmd, body=%wide.region_6.7_spmd.sunk | while | flops 131077 | bytes 786615 | solution.py:19
  354.2 1.1 bitcast_add_fusion.4
  355.3 1.1 bitcast_add_fusion.4
  356.4 1.1 bitcast_add_fusion.4
  357.5 1.1 bitcast_add_fusion.4
  358.6 1.1 bitcast_add_fusion.4
  359.7 1.1 bitcast_add_fusion.4
  360.8 1.1 bitcast_add_fusion.4
  364.1 1.1 bitcast_add_fusion.4
  365.2 1.1 bitcast_add_fusion.4
  366.3 1.1 bitcast_add_fusion.4
  367.4 1.1 bitcast_add_fusion.4
  368.5 1.1 bitcast_add_fusion.4
  369.6 1.1 bitcast_add_fusion.4
  375.2 1.1 bitcast_add_fusion.4
  376.3 1.1 bitcast_add_fusion.4
  377.4 1.1 bitcast_add_fusion.4
  378.5 1.1 bitcast_add_fusion.4
  379.6 1.1 bitcast_add_fusion.4
  380.7 1.1 bitcast_add_fusion.4
  385.1 1.1 bitcast_add_fusion.4
  386.2 1.1 bitcast_add_fusion.4
  387.3 1.1 bitcast_add_fusion.4
  388.4 1.1 bitcast_add_fusion.4
  389.5 1.1 bitcast_add_fusion.4
  390.6 1.1 bitcast_add_fusion.4
  396.1 1.1 bitcast_add_fusion.4
  397.2 1.1 bitcast_add_fusion.4
  398.3 1.1 bitcast_add_fusion.4
  399.4 1.1 bitcast_add_fusion.4
  400.5 1.1 bitcast_add_fusion.4
  401.6 1.1 bitcast_add_fusion.4
  406.1 1.1 bitcast_add_fusion.4
  407.2 1.1 bitcast_add_fusion.4
  408.3 1.1 bitcast_add_fusion.4
  409.4 1.1 bitcast_add_fusion.4
  410.5 1.1 bitcast_add_fusion.4
  411.6 1.1 bitcast_add_fusion.4
  417.1 1.1 bitcast_add_fusion.4
  418.2 1.1 bitcast_add_fusion.4
  419.3 1.1 bitcast_add_fusion.4
  420.4 1.1 bitcast_add_fusion.4
  421.5 1.1 bitcast_add_fusion.4
  422.6 1.1 bitcast_add_fusion.4
  424.0 14.2 %while.36 = (s32[]{:T(128)}, bf16[2,512,4,128]{3,2,1,0:T(4,128)(2,1)}, bf16[2,512,4,128]{1,3,2,0:T(8,128)(2,1)}, f32[2,512,4]{1,2,0:T(4,128)S(1)}, bf16[2,512,4,...) while((s32[]{:T(128)}, ...), condition=%wide.region_12.13_spmd, body=%wide.region_8.12_spmd.sunk | while | flops 945817664 | bytes 9857989 | solution.py:94
  424.0 1.2 reduce-window.24
  425.8 3.1 fusion.46
  431.1 1.2 reduce-window.24
  432.9 3.1 fusion.46
  438.2 2.4 copy.70
  (156 shorter events, 32.3 us)
Async XLA Ops:
  6.5 1.5 copy-start.5
  6.5 88.4 %all-gather.8.cloned.1.call-start = ((), (), s32[]{:S(2)}) async-start(), calls=%async_computation.1 | async-start | bytes 10485760 | tf_op jit(solution)/shard_map/all_gather | solution.py:74
  7.3 178.6 %all-gather.6.cloned.1.call-start = ((), (), s32[]{:S(2)}) async-start(), calls=%async_computation | async-start | bytes 12779520 | tf_op jit(solution)/shard_map/all_gather | solution.py:88
  8.0 346.1 %all-gather.10.cloned.1.call-start = ((), (), s32[]{:S(2)}) async-start(), calls=%async_computation.2 | async-start | bytes 17039360 | tf_op jit(solution)/shard_map/all_gather | solution.py:11
  220.3 2.8 copy-start.1
  223.1 2.8 copy-start.3
  223.1 2.8 copy-start.4
  225.9 1.2 copy-start.6
  225.9 127.1 %copy-start.2 = (bf16[2,512,4,128]{1,0,3,2:T(2,128)(2,1)S(1)}, bf16[2,512,4,128]{1,0,3,2:T(2,128)(2,1)}, u32[]{:S(2)}) copy-start(bf16[2,512,4,128]{1,0,3,2:T(2,128)(2,1)} %convert_element_type.24) | copy-start | bytes 3145732
  226.3 0.7 copy-start
Sparse Core Ops, SparseCore 0:
  9.2 85.7 all-gather.7
  97.8 88.0 all-gather.5
  227.1 96.5 all-gather.9
where the time goes:
time: 449 us; the launch traced here: 447 us
  waiting for transfers between devices  176 us (39%)
  blocking collectives  125 us (28%)
  other arithmetic  76.6 us (17%)
  matrix products  27.7 us (6%)
  local copies, waits for them, and re-layouts  26.2 us (6%)
  between operations  13.9 us (3%)
    unnamed x1, blocking collectives  125 us
    all_gather x1, waiting for transfers between devices, on_device(): lax.all_gather(projection, 'seq', axis=1, tiled=True)  90.9 us
    all_gather x1, waiting for transfers between devices, on_device(): features = lax.all_gather(tokens, 'fsdp', axis=1, tiled=True)  83.5 us
    add x63, other arithmetic, combine(): later[0][:, None, None] * earlier[1] + later[1]  66.8 us
    dot_general x1, matrix products, on_device(): jnp.einsum('td,cdn->ctn', features, lax.all_gather(projection, 'seq', axi...  17.3 us
  transfers between devices with their start and end apart: 3, of which 2 were waited for; matrix products, arithmetic and copies ran while one was open for 1% of the time, Pallas kernels for 0%

commit v1 on v0

--- a/solution.py
+++ b/solution.py
@@ -71,7 +71,10 @@
 
 
 def on_device(tokens, projection, log_decay):
-    features = lax.all_gather(tokens, "fsdp", axis=1, tiled=True)
+    size = lax.axis_size("fsdp")
+    pieces = jnp.stack([tokens for _ in range(size)])
+    pieces = lax.all_to_all(pieces, "fsdp", split_axis=0, concat_axis=0)
+    features = jnp.concatenate(pieces, axis=1)
     rows = features.shape[0]
     heads = log_decay.shape[1]
     width = projection.shape[2]

time: 449 us -> 403 us (0.90)
  waiting for transfers between devices: 176 us -> 90.5 us
  local copies, waits for them, and re-layouts: 26.2 us -> 58.7 us
  starting transfers between devices: 0.08 us -> 5.84 us
    all_gather x1, waiting for transfers between devices: 90.9 us -> 0.01 us  [on_device(): lax.all_gather(projection, 'seq', axis=1, tiled=True)]
    all_to_all x0 -> x1, waiting for transfers between devices: none -> 89.7 us  [on_device(): pieces = lax.all_to_all(pieces, 'fsdp', split_axis=0, concat_axis=0)]
    all_gather x1 -> x0, waiting for transfers between devices: 83.5 us -> none  [on_device(): features = lax.all_gather(tokens, 'fsdp', axis=1, tiled=True)]
    reshape x2 -> x4, local copies, waits for them, and re-layouts: 0.03 us -> 26.6 us  [the longest x2 26.6 us: on_device(): features = jnp.concatenate(pieces, axis=1)]
    another operation x4 -> x5, local copies, waits for them, and re-layouts: 0.22 us -> 6.29 us  [the longest x1 6.07 us: on_device(): pieces = jnp.stack([tokens for _ in range(size)])]
    all_to_all x0 -> x1, starting transfers between devices: none -> 5.79 us  [on_device(): pieces = lax.all_to_all(pieces, 'fsdp', split_axis=0, concat_axis=0)]
  transfers between devices with their start and end apart: 3 -> 3, of which waited for: 2 -> 1; matrix products, arithmetic and copies ran while one was open for 1% -> 9% of each run, Pallas kernels for 0% -> 0%
where the time goes in v1:
time: 403 us; the launch traced here: 401 us
  blocking collectives  124 us (31%)
  waiting for transfers between devices  90.5 us (22%)
  other arithmetic  76.6 us (19%)
  local copies, waits for them, and re-layouts  58.7 us (15%)
  matrix products  27.7 us (7%)
  between operations  14.3 us (4%)
  starting transfers between devices  5.84 us (1%)
    unnamed x1, blocking collectives  124 us
    all_to_all x1, waiting for transfers between devices, on_device(): pieces = lax.all_to_all(pieces, 'fsdp', split_axis=0, concat_axis=0)  89.7 us
    add x63, other arithmetic, combine(): later[0][:, None, None] * earlier[1] + later[1]  66.8 us
    reshape x2, local copies, waits for them, and re-layouts, on_device(): features = jnp.concatenate(pieces, axis=1)  26.6 us
    dot_general x1, matrix products, on_device(): jnp.einsum('td,cdn->ctn', features, lax.all_gather(projection, 'seq', axi...  17.3 us
    squeeze x2, local copies, waits for them, and re-layouts, on_device(): key_vecs, value_vecs, incoming = chain(raw[1], raw[2], decay, shaped)  8.14 us
  transfers between devices with their start and end apart: 3, of which 1 were waited for; matrix products, arithmetic and copies ran while one was open for 9% of the time, Pallas kernels for 0%

profile of v1, /device:TPU:249, one launch (start us, length us, event | category | flops | bytes accessed | tf_op | source)
XLA Modules:
  0.0 400.6 jit_solution(9774965457901973969)
XLA Ops:
  7.3 6.1 %stack.2 = bf16[4,1024,1024]{2,1,0:T(8,128)(2,1)} broadcast(bf16[1024,1024]{1,0:T(8,128)(2,1)} %param.9), dimensions={1,2} | broadcast | bytes 10485760 | tf_op jit(solution)/shard_map/stack | solution.py:75
  13.3 5.8 %all-to-all-start = ((bf16[4,1024,1024]{2,1,0:T(8,128)(2,1)}), bf16[4,1024,1024]{2,1,0:T(8,128)(2,1)}, u32[]{:S(2)}, u32[]{:S(2)}) async-start(bf16[4,1024,1024]{2,1,0:T(8,128)(2,1)} %stack.2), calls=%async_computation | async-start | bytes 16777216 | tf_op jit(solution)/shard_map/all_to_all | solution.py:76
  19.2 2.4 reduce-window.14
  22.6 89.7 %all-to-all-done = bf16[4,1024,1024]{2,1,0:T(8,128)(2,1)} async-done(((bf16[4,1024,1024]{2,1,0:T(8,128)(2,1)}), bf16[4,1024,1024]{2,1,0:T(8,128)(2,1)}, u32[]{:S(2)}, u32[]{:S(2)}) %all-to-all-start) | async-done | bytes 8388640 | tf_op jit(solution)/shard_map/all_to_all | solution.py:76
  112.3 12.1 %copy.50 = bf16[1024,4,1024]{2,1,0:T(4,128)(2,1)} copy(bf16[1024,4,1024]{2,0,1:T(8,128)(2,1)} %bitcast.12) | data formatting | bytes 16777216 | tf_op jit(solution)/shard_map/reshape | solution.py:77
  124.5 14.4 %reshape.127 = bf16[1024,4096,1]{1,0,2:T(8,128)(2,1)} reshape(bf16[1024,4,1024]{2,1,0:T(4,128)(2,1)} %copy.50) | data formatting | bytes 16777216 | tf_op jit(solution)/shard_map/reshape | solution.py:77
  138.9 17.3 %convolution_bitcast_fusion.1 = f32[3,1024,512]{1,2,0:T(8,128)S(1)} fusion(bf16[3,4096,512]{2,1,0:T(8,128)(2,1)} %all-gather.5.cloned.1.call-done, bf16[1024,4096,1]{1,0,2:T(8,128)(2,1)} %reshape.127), kind=kOutput, calls=%fused_computation.37 | convolution fusion | flops 12884901888 | bytes 27262976 | tf_op jit(solution)/shard_map/td,cdn->ctn/dot_general | solution.py:88
  156.2 1.8 fusion.30
  158.1 2.8 squeeze.41
  160.9 2.8 copy.52
  163.7 4.0 squeeze.42
  167.7 4.1 %copy.54 = f32[2,512,4,128]{3,1,2,0:T(8,128)} copy(f32[2,512,4,128]{1,0,3,2:T(2,128)} %squeeze.42) | data formatting | bytes 4194304 | tf_op jit(solution)/shard_map/squeeze | solution.py:94
  171.8 1.6 convert_element_type.24
  173.4 2.8 multiply_convert_fusion.2
  176.2 2.7 fusion.25
  181.4 124.5 %all-reduce = f32[256]{0:T(256)S(1)} all-reduce(f32[256]{0:T(256)S(1)} %exponential_dynamic-update-slice_fusion), channel_id=2, replica_groups=mesh['seq'=64,'fsdp'=4] {'seq'}, use_global_device_ids=true, to_apply=%add | all-reduce | flops 256 | bytes 2048
  306.0 1.2 copy.57
  307.2 69.9 %while.35 = (s32[]{:T(128)}, f32[4,128,128]{2,1,0:T(8,128)S(1)}, s32[]{:T(128)}, f32[64,4]{1,0:T(8,128)S(1)}, f32[64,4,128,128]{3,2,1,0:T(8,128)}, /*index=5*/s32[]{:T(128)}, s32[]{:T(128)}, s32[]{:T(128)}) while((s32[]{:T(128)}, f32[4,128,128]{2,1,0:T(8,128)S(1)}, s32[]{:T(128)}, f32[64,4]{1,0:T(8,128)S(1)}, f32[64,4,128,128]{3,2,1,0:T(8,128)}, ...), condition=%wide.region_7.8_spmd, body=%wide.region_6.7_spmd.sunk | while | flops 131077 | bytes 786607 | solution.py:19
  307.2 1.1 bitcast_add_fusion.4
  308.4 1.1 bitcast_add_fusion.4
  309.5 1.1 bitcast_add_fusion.4
  311.7 1.1 bitcast_add_fusion.4
  313.9 1.1 bitcast_add_fusion.4
  316.1 1.1 bitcast_add_fusion.4
  318.3 1.1 bitcast_add_fusion.4
  319.4 1.1 bitcast_add_fusion.4
  320.5 1.1 bitcast_add_fusion.4
  321.6 1.1 bitcast_add_fusion.4
  322.7 1.1 bitcast_add_fusion.4
  323.8 1.1 bitcast_add_fusion.4
  326.0 1.1 bitcast_add_fusion.4
  328.3 1.1 bitcast_add_fusion.4
  330.5 1.1 bitcast_add_fusion.4
  332.7 1.1 bitcast_add_fusion.4
  334.9 1.1 bitcast_add_fusion.4
  337.1 1.1 bitcast_add_fusion.4
  339.3 1.1 bitcast_add_fusion.4
  340.4 1.1 bitcast_add_fusion.4
  341.5 1.1 bitcast_add_fusion.4
  342.6 1.1 bitcast_add_fusion.4
  343.7 1.1 bitcast_add_fusion.4
  344.8 1.1 bitcast_add_fusion.4
  347.1 1.1 bitcast_add_fusion.4
  349.3 1.1 bitcast_add_fusion.4
  351.5 1.1 bitcast_add_fusion.4
  353.7 1.1 bitcast_add_fusion.4
  355.9 1.1 bitcast_add_fusion.4
  358.1 1.1 bitcast_add_fusion.4
  360.3 1.1 bitcast_add_fusion.4
  361.4 1.1 bitcast_add_fusion.4
  362.5 1.1 bitcast_add_fusion.4
  363.6 1.1 bitcast_add_fusion.4
  364.7 1.1 bitcast_add_fusion.4
  365.9 1.1 bitcast_add_fusion.4
  368.1 1.1 bitcast_add_fusion.4
  370.3 1.1 bitcast_add_fusion.4
  372.5 1.1 bitcast_add_fusion.4
  374.7 1.1 bitcast_add_fusion.4
  377.2 14.2 %while.36 = (s32[]{:T(128)}, bf16[2,512,4,128]{3,2,1,0:T(4,128)(2,1)}, bf16[2,512,4,128]{1,3,2,0:T(8,128)(2,1)}, f32[2,512,4]{1,2,0:T(4,128)S(1)}, bf16[2,512,4,...) while((s32[]{:T(128)}, ...), condition=%wide.region_12.13_spmd, body=%wide.region_8.12_spmd.sunk | while | flops 945817664 | bytes 9858489 | solution.py:97
  377.2 1.2 reduce-window.24
  379.0 3.1 fusion.42
  384.3 1.2 reduce-window.24
  386.0 3.1 fusion.42
  391.4 2.4 copy.73
  (158 shorter events, 34.6 us)
Async XLA Ops:
  6.5 132.4 %all-gather.5.cloned.1.call-start = ((), (), s32[]{:S(2)}) async-start(), calls=%async_computation.1 | async-start | bytes 12779520 | tf_op jit(solution)/shard_map/all_gather | solution.py:91
  13.3 5.9 %copy-start.5 = (f32[1024,4]{0,1:T(4,128)S(1)}, f32[1024,4]{0,1:T(4,128)}, u32[]{:S(2)}) copy-start(f32[1024,4]{0,1:T(4,128)} %param.11) | copy-start | bytes 49156
  13.3 99.0 %all-to-all-start = ((bf16[4,1024,1024]{2,1,0:T(8,128)(2,1)}), bf16[4,1024,1024]{2,1,0:T(8,128)(2,1)}, u32[]{:S(2)}, u32[]{:S(2)}) async-start(bf16[4,1024,1024]{2,1,0:T(8,128)(2,1)} %stack.2), calls=%async_computation | async-start | bytes 16777216 | tf_op jit(solution)/shard_map/all_to_all | solution.py:76
  19.1 288.1 %all-gather.7.cloned.1.call-start = ((), (), s32[]{:S(2)}) async-start(), calls=%async_computation.2 | async-start | bytes 17039360 | tf_op jit(solution)/shard_map/all_gather | solution.py:11
  173.4 2.8 copy-start.1
  176.1 2.8 copy-start.3
  176.1 2.8 copy-start.4
  178.9 1.2 copy-start.6
  178.9 127.1 %copy-start.2 = (bf16[2,512,4,128]{1,0,3,2:T(2,128)(2,1)S(1)}, bf16[2,512,4,128]{1,0,3,2:T(2,128)(2,1)}, u32[]{:S(2)}) copy-start(bf16[2,512,4,128]{1,0,3,2:T(2,128)(2,1)} %convert_element_type.24) | copy-start | bytes 3145732
  179.3 0.7 copy-start
Sparse Core Ops, SparseCore 0:
  10.2 87.2 all-gather.4
  180.1 95.8 all-gather.6
